TPU v7x, 32 devices: a whole 2x2x4 slice. The times are simulated.
32 devices in a mesh: groups: 2 (over y), feat: 16 (over z, x, core).
Axes of the slice: x: 2, y: 2, z: 4, core: 2. Of those that a mesh axis runs over, the one named last changes fastest.
Arguments:
- residual: bfloat16 [2, 256, 8192], P(None, ('groups', 'feat')), parts along dimension 1, may hold values from -6 to 6
- feature_ids: int32 [2, 256, 64], P(None, 'groups'), parts along dimension 1, may hold values from 0 to 2047, as said below
- activations: bfloat16 [2, 256, 64], P(None, 'groups'), parts along dimension 1, may hold values from 0.5 to 8
- decoder: bfloat16 [4096, 8192], P(('groups', 'feat')), parts along dimension 0, may hold values from -0.0625 to 0.0625
- bias: bfloat16 [16384], P('groups'), parts along dimension 0, may hold values from -5 to 5
Outputs:
- weight_grad: bfloat16 [4096, 8192], P(('groups', 'feat')), parts along dimension 0
- code_grad: float32 [2, 256, 64], P(None, 'groups'), parts along dimension 1
There are 2 independent parts, one for each index of `groups`. A program takes and returns all parts, laid end to end along the dimension named above; each array names one. Nothing has to cross between parts.
Inputs may be any that keep to these rules, and one draw needn't show every extreme that they name: `feature_ids`: each token's 64 feature numbers are distinct; both ends of the range are used. `feature_ids`: in each micro-batch, the 512 feature numbers of the tokens i * 8 to (i + 1) * 8 - 1 are distinct, and at most 64 of them lie in one run of 128 numbers f * 128 to (f + 1) * 128 - 1; every such group of tokens reaches 64 in some run.
All inputs are finite; a program needn't handle non-finite values.
Results may differ from a plain program's by a relative error of at most 0.0034.
Values may be sent and summed in bfloat16 or wider, within the bound.
A program may use at most 64 MiB of HBM per device.

v0:
```python
import jax
import jax.numpy as jnp
from jax import lax
from jax.sharding import PartitionSpec as P


def local_codes(ids_block, acts_block, first_feature, feat_count):
    matches = (ids_block - first_feature)[:, :, None] == lax.iota(jnp.int32, feat_count)[
        None, None, :
    ]
    dense = jnp.einsum(
        "tkf,tk->tf", matches.astype(jnp.bfloat16), acts_block, preferred_element_type=jnp.float32
    )
    return dense.astype(jnp.bfloat16)


def pick_owned(backward, ids_block, first_feature, feat_count):
    local_ids = ids_block - first_feature
    owned = (local_ids >= 0) & (local_ids < feat_count)
    taken = jnp.take_along_axis(backward, jnp.clip(local_ids, 0, feat_count - 1), axis=1)
    return jnp.where(owned, taken, jnp.float32(0.0))


def error_products(codes, errors_all, decoder):
    weight_term = jnp.einsum("tf,td->fd", codes, errors_all, preferred_element_type=jnp.float32)
    backward = jnp.einsum("td,fd->tf", errors_all, decoder, preferred_element_type=jnp.float32)
    return (weight_term, backward)


def local(residual, feature_ids, activations, decoder, bias):
    feat_count, model_width = decoder.shape
    batches, share_rows = (residual.shape[0], residual.shape[1])
    first_feature = lax.axis_index("feat") * feat_count
    bias_wide = bias.astype(jnp.float32)
    accum = jnp.zeros((feat_count, model_width), jnp.float32)
    codes_list = [
        local_codes(feature_ids[batch], activations[batch], first_feature, feat_count)
        for batch in range(batches)
    ]
    picks = []
    for batch in range(batches):
        codes = codes_list[batch]

        def project(begin, number, codes=codes):
            return jnp.dot(codes, decoder, preferred_element_type=jnp.float32)

        recon = lax.psum_scatter(
            project(jnp.int32(0), share_rows * lax.axis_size("feat")),
            "feat",
            scatter_dimension=0,
            tiled=True,
        )
        error_share = (recon + bias_wide - residual[batch].astype(jnp.float32)).astype(jnp.bfloat16)
        errors_all = lax.all_gather(error_share, "feat", axis=0, tiled=True)
        weight_term, backward = error_products(codes, errors_all, decoder)
        accum = accum + weight_term
        picks.append(pick_owned(backward, feature_ids[batch], first_feature, feat_count))
    code_grad = lax.psum(jnp.stack(picks), "feat")
    return (accum.astype(jnp.bfloat16), code_grad)


def solution(mesh):
    placed = (
        P(None, ("groups", "feat"), None),
        P(None, "groups", None),
        P(None, "groups", None),
        P(("groups", "feat"), None),
        P("groups"),
    )
    return jax.shard_map(
        local,
        mesh=mesh,
        in_specs=placed,
        out_specs=(P(("groups", "feat"), None), P(None, "groups", None)),
        check_vma=False,
    )
```

profile of v0, /device:TPU:0, one launch (start us, length us, event | category | flops | bytes accessed | tf_op | source)
XLA Modules:
  0.0 408.5 jit_solution(9860008641075383409)
XLA Ops:
  7.2 0.0 copy-start
  7.2 0.0 reduce-scatter.3.cloned.1.call-start
  7.2 0.9 slice_bitcast_fusion
  8.1 0.1 copy.12
  8.2 0.8 fusion.16
  9.0 0.1 copy.17
  9.1 0.1 copy.16
  9.2 0.1 bitcast_or_fusion
  9.3 1.8 fusion.1
  11.1 0.0 copy-done
  11.1 2.7 fusion.14
  13.8 0.0 reduce-scatter.3.cloned.1.call-update
  13.8 0.0 reduce-scatter.5.cloned.1.call-start
  13.9 0.1 copy.14
  14.0 1.8 fusion.2
  15.8 0.0 copy-start.3
  15.8 0.0 copy-start.2
  15.8 2.7 fusion.10
  18.5 0.0 reduce-scatter.5.cloned.1.call-update
  18.5 0.0 all-gather.3.cloned.1.call-start
  18.6 0.0 copy-done.3
  18.6 70.4 %reduce-scatter.3.cloned.1.call-done = f32[8,8192]{1,0:T(8,128)} async-done(((f32[128,8192]{1,0:T(8,128)}), f32[8,8192]{1,0:T(8,128)}) %reduce-scatter.3.cloned.1.call-update) | async-done | bytes 262160 | tf_op jit(solution)/shard_map/reduce_scatter | solution.py:47
  89.0 75.8 %reduce-scatter.5.cloned.1.call-done = f32[8,8192]{1,0:T(8,128)} async-done(((f32[128,8192]{1,0:T(8,128)}), f32[8,8192]{1,0:T(8,128)}) %reduce-scatter.5.cloned.1.call-update) | async-done | bytes 262160 | tf_op jit(solution)/shard_map/reduce_scatter | solution.py:47
  164.8 0.0 copy-done.2
  164.8 1.8 fusion.5
  166.6 0.0 all-gather.3.cloned.1.call-update
  166.7 0.0 all-gather.5.cloned.1.call-start
  166.7 0.5 all-gather.5.cloned.1.call-update
  167.2 0.0 all-reduce.2.cloned.1.call-start
  167.3 0.1 reshape.62
  167.4 0.1 reshape.57
  167.4 40.1 %all-gather.3.cloned.1.call-done = bf16[128,8192]{1,0:T(8,128)(2,1)} async-done(((bf16[8,8192]{1,0:T(8,128)(2,1)}), bf16[128,8192]{1,0:T(8,128)(2,1)}) %all-gather.3.cloned.1.call-update) | async-done | bytes 2097168 | tf_op jit(solution)/shard_map/all_gather | solution.py:54
  207.5 2.3 fusion.17
  209.8 50.7 %gather_fusion = f32[8192]{0:T(1024)S(1)} fusion(f32[128,128]{1,0:T(8,128)S(1)} %fusion.17, s32[8192]{0:T(1024)S(1)} %reshape.57), kind=kCustom, calls=%fused_computation.clone | custom fusion | bytes 131072 | tf_op jit(solution)/shard_map/jit(take_along_axis)/gather | solution.py:20
  260.5 0.1 reshape.60
  260.6 0.0 all-gather.5.cloned.1.call-done
  260.7 2.3 fusion.18
  263.0 50.7 %gather_fusion.1 = f32[8192]{0:T(1024)S(1)} fusion(f32[128,128]{1,0:T(8,128)S(1)} %fusion.18, s32[8192]{0:T(1024)S(1)} %reshape.62), kind=kCustom, calls=%fused_computation.1.clone | custom fusion | bytes 131072 | tf_op jit(solution)/shard_map/jit(take_along_axis)/gather | solution.py:20
  313.7 0.1 reshape.65
  313.8 0.7 pad_maximum_fusion
  314.5 0.0 all-reduce.2.cloned.1.call-update
  314.5 0.0 copy-start.1
  314.5 2.5 fusion.12
  317.0 0.0 copy-done.1
  317.0 2.1 fusion
  319.1 81.3 %all-reduce.2.cloned.1.call-done = f32[2,128,64]{2,1,0:T(8,128)} async-done(((f32[2,128,64]{2,1,0:T(8,128)}), f32[2,128,64]{2,1,0:T(8,128)}) %all-reduce.2.cloned.1.call-update) | async-done | bytes 65552 | tf_op jit(solution)/shard_map/psum | solution.py:58
  400.4 1.6 copy.11
  (3 shorter events, 0.1 us)
Async XLA Ops:
  7.2 4.0 copy-start
  7.2 81.8 %reduce-scatter.3.cloned.1.call-start = ((), (), s32[]{:S(2)}) async-start(), calls=%async_computation.2 | async-start | bytes 4456448 | tf_op jit(solution)/shard_map/reduce_scatter | solution.py:47
  13.8 151.0 %reduce-scatter.5.cloned.1.call-start = ((), (), s32[]{:S(2)}) async-start(), calls=%async_computation.4 | async-start | bytes 4456448 | tf_op jit(solution)/shard_map/reduce_scatter | solution.py:47
  15.8 2.8 copy-start.3
  15.8 149.0 %copy-start.2 = (bf16[2,8,8192]{2,1,0:T(8,128)(2,1)S(1)}, bf16[2,8,8192]{2,1,0:T(8,128)(2,1)}, u32[]{:S(2)}) copy-start(bf16[2,8,8192]{2,1,0:T(8,128)(2,1)} %param.7) | copy-start | bytes 786436
  18.5 189.0 %all-gather.3.cloned.1.call-start = ((), (), s32[]{:S(2)}) async-start(), calls=%async_computation.3 | async-start | bytes 2228224 | tf_op jit(solution)/shard_map/all_gather | solution.py:54
  166.7 94.0 %all-gather.5.cloned.1.call-start = ((), (), s32[]{:S(2)}) async-start(), calls=%async_computation.5 | async-start | bytes 2228224 | tf_op jit(solution)/shard_map/all_gather | solution.py:54
  167.2 233.2 %all-reduce.2.cloned.1.call-start = ((), (), s32[]{:S(2)}) async-start(), calls=%async_computation.6 | async-start | bytes 262144 | tf_op jit(solution)/shard_map/psum | solution.py:58
  314.5 2.5 copy-start.1
Sparse Core Ops, SparseCore 0:
  13.9 75.0 reduce-scatter.2
  93.4 71.4 reduce-scatter.4
  167.0 40.4 all-gather.2
  210.1 40.1 all-gather.4
  314.6 85.7 all-reduce.1
where the time goes:
time: 410 us; the launch traced here: 409 us
  waiting for transfers between devices  268 us (65%)
  local copies, waits for them, and re-layouts  105 us (26%)
  matrix products  18.1 us (4%)
  between operations  13.9 us (3%)
    reduce_scatter x2, waiting for transfers between devices, local(): lax.psum_scatter(project(jnp.int32(0), share_rows * lax.axis_size('feat')...  146 us
    gather x6, local copies, waits for them, and re-layouts, pick_owned(): jnp.take_along_axis(backward, jnp.clip(local_ids, 0, feat_count - 1), axi...  102 us
    psum x1, waiting for transfers between devices, local(): code_grad = lax.psum(jnp.stack(picks), 'feat')  81.3 us
    all_gather x2, waiting for transfers between devices, local(): errors_all = lax.all_gather(error_share, 'feat', axis=0, tiled=True)  40.1 us
  transfers between devices with their start and end apart: 5, of which 4 were waited for; matrix products, arithmetic and copies ran while one was open for 15% of the time, Pallas kernels for 0%

commit v1 on v0

--- a/solution.py
+++ b/solution.py
@@ -1,7 +1,365 @@
 import jax
 import jax.numpy as jnp
 from jax import lax
+from jax.experimental import pallas as pl
+from jax.experimental.pallas import tpu as pltpu
 from jax.sharding import PartitionSpec as P
+
+MESH = pl.DeviceIdType.MESH
+PLANES = 4
+QUARTERS = 4
+DEVICES = PLANES * QUARTERS
+CHUNKS = 4
+SUM_TYPE = jnp.float32
+
+
+def fused_kernel(
+    ids_ref,
+    acts_ref,
+    res_ref,
+    dec_in,
+    bias_ref,
+    wg_out,
+    cg_out,
+    dec,
+    part,
+    got1,
+    got2,
+    err,
+    wg,
+    res,
+    codes,
+    codes_t,
+    back,
+    pick,
+    cg_got,
+    own_sem,
+    dec_send,
+    dec_recv,
+    res_send,
+    res_recv,
+    sum_send,
+    sum_recv,
+    wg_send,
+    wg_recv,
+    wg_own,
+    cg_send,
+    cg_recv,
+):
+    feat = dec_in.shape[0]
+    width = dec_in.shape[1] // QUARTERS
+    step = width // CHUNKS
+    tokens = codes.shape[0]
+    half, quarter = tokens // 2, tokens // 4
+    share = res_ref.shape[0]
+    lanes = ids_ref.shape[1]
+    top_k = lanes // 2
+    rows8 = share // 2
+
+    me = lax.axis_index("feat")
+    z, q = lax.div(me, QUARTERS), lax.rem(me, QUARTERS)
+    z_hi, z_lo = lax.div(z, 2), lax.rem(z, 2)
+    near = (z + 1 - 2 * z_lo) * QUARTERS + q
+    far = lax.rem(z + 2, PLANES) * QUARTERS + q
+    mates = [lax.rem(q + r, QUARTERS) for r in range(QUARTERS)]
+
+    def span(start, size):
+        return pl.ds(pl.multiple_of(start, size), size)
+
+    def remote(src, dst, send, recv, device):
+        copy = pltpu.make_async_remote_copy(
+            src_ref=src,
+            dst_ref=dst,
+            send_sem=send,
+            recv_sem=recv,
+            device_id={"feat": device},
+            device_id_type=MESH,
+        )
+        copy.start()
+        return copy
+
+    barrier = pltpu.get_barrier_semaphore()
+    for r in range(1, DEVICES):
+        pl.semaphore_signal(
+            barrier, inc=1, device_id={"feat": lax.rem(me + r, DEVICES)}, device_id_type=MESH
+        )
+    pl.semaphore_wait(barrier, DEVICES - 1)
+
+    sends = []
+    own_dec = pltpu.make_async_copy(
+        dec_in.at[:, span(q * width, width)], dec.at[span(q * feat, feat), :], own_sem.at[0]
+    )
+    own_dec.start()
+    own_res = pltpu.make_async_copy(
+        res_ref.at[:, span(q * width, width)], res.at[span(q * share, share), :], own_sem.at[1]
+    )
+    own_res.start()
+    dec_copies = {}
+    res_copies = []
+    for c in range(CHUNKS):
+        for r in range(1, QUARTERS):
+            dec_copies[c, r] = remote(
+                dec_in.at[:, span(mates[r] * width + c * step, step)],
+                dec.at[span(q * feat, feat), pl.ds(c * step, step)],
+                dec_send.at[c, r],
+                dec_recv.at[c, r],
+                z * QUARTERS + mates[r],
+            )
+        if c == 0:
+            for r in range(1, QUARTERS):
+                res_copies.append(
+                    remote(
+                        res_ref.at[:, span(mates[r] * width, width)],
+                        res.at[span(q * share, share), :],
+                        res_send.at[r],
+                        res_recv.at[r],
+                        z * QUARTERS + mates[r],
+                    )
+                )
+    sends += list(dec_copies.values()) + res_copies
+
+    plane_feat = QUARTERS * feat
+    first = z * plane_feat
+
+    def row_of(i):
+        zi, qi = lax.div(i, QUARTERS), lax.rem(i, QUARTERS)
+        return pl.multiple_of((lax.rem(zi, 2) * 2 + lax.div(zi, 2)) * quarter + qi * share, share)
+
+    @pl.loop(0, DEVICES)
+    def _(i):
+        rows = pl.ds(pl.multiple_of(i * rows8, rows8), rows8)
+        ids8 = ids_ref[rows, :] - first
+        acts8 = acts_ref[rows, :]
+        feature = lax.broadcasted_iota(jnp.int32, (rows8, plane_feat), 1)
+        blocks = []
+        for batch in range(2):
+            block = jnp.zeros((rows8, plane_feat), jnp.float32)
+            for k in range(batch * top_k, (batch + 1) * top_k):
+                block = jnp.where(ids8[:, k : k + 1] == feature, acts8[:, k : k + 1], block)
+            blocks.append(block)
+        both = jnp.concatenate(blocks, axis=0)
+        codes[pl.ds(row_of(i), share), :] = both.astype(jnp.bfloat16)
+
+    for f in range(QUARTERS):
+        codes_t[f * feat : (f + 1) * feat, :] = (
+            codes[:, f * feat : (f + 1) * feat].astype(jnp.float32).T.astype(jnp.bfloat16)
+        )
+
+    own_dec.wait()
+    own_res.wait()
+
+    mine_half = span(z_lo * half, half)
+    other_half = span((1 - z_lo) * half, half)
+    mine = span(z_lo * half + z_hi * quarter, quarter)
+    other = span(z_lo * half + (1 - z_hi) * quarter, quarter)
+    flying = {}
+
+    def cols_of(c):
+        return pl.ds(c * step, step)
+
+    def project(c):
+        cols = cols_of(c)
+        for r in range(1, QUARTERS):
+            dec_copies[c, r].wait_recv()
+        part[:, cols] = jnp.dot(
+            codes[...], dec[:, cols], preferred_element_type=jnp.float32
+        ).astype(part.dtype)
+        flying[0, c] = remote(
+            part.at[other_half, cols], got1.at[:, cols], sum_send.at[0, c], sum_recv.at[0, c], near
+        )
+
+    def halve(c):
+        cols = cols_of(c)
+        flying[0, c].wait_recv()
+        part[mine_half, cols] = part[mine_half, cols] + got1[:, cols]
+        flying[1, c] = remote(
+            part.at[other, cols], got2.at[:, cols], sum_send.at[1, c], sum_recv.at[1, c], far
+        )
+
+    def make_error(c):
+        cols = cols_of(c)
+        if c == 0:
+            for copy in res_copies:
+                copy.wait_recv()
+        flying[1, c].wait_recv()
+        recon = part[mine, cols] + got2[:, cols]
+        shift = bias_ref[:, span(q * width + c * step, step)]
+        err[mine, cols] = (recon + shift - res[:, cols].astype(jnp.float32)).astype(jnp.bfloat16)
+        flying[2, c] = remote(
+            err.at[mine, cols], err.at[mine, cols], sum_send.at[2, c], sum_recv.at[2, c], far
+        )
+
+    def spread(c):
+        cols = cols_of(c)
+        flying[2, c].wait_recv()
+        flying[3, c] = remote(
+            err.at[mine_half, cols],
+            err.at[mine_half, cols],
+            sum_send.at[3, c],
+            sum_recv.at[3, c],
+            near,
+        )
+
+    wg_copies = []
+    wg_local = []
+
+    def gradients(c):
+        cols = cols_of(c)
+        flying[3, c].wait_recv()
+        wg[:, cols] = jnp.dot(
+            codes_t[...], err[:, cols], preferred_element_type=jnp.float32
+        ).astype(jnp.bfloat16)
+        place = span(q * width + c * step, step)
+        for r in range(1, QUARTERS):
+            wg_copies.append(
+                remote(
+                    wg.at[span(mates[r] * feat, feat), cols],
+                    wg_out.at[:, place],
+                    wg_send.at[c, r],
+                    wg_recv.at[c, r],
+                    z * QUARTERS + mates[r],
+                )
+            )
+        local = pltpu.make_async_copy(
+            wg.at[span(q * feat, feat), cols], wg_out.at[:, place], wg_own.at[c]
+        )
+        local.start()
+        wg_local.append(local)
+        term = lax.dot_general(
+            err[:, cols],
+            dec[:, cols],
+            (((1,), (1,)), ((), ())),
+            preferred_element_type=jnp.float32,
+        )
+        back[...] = term if c == 0 else back[...] + term
+
+    stages = (project, halve, make_error, spread, gradients)
+    for tick in range(CHUNKS + len(stages) - 1):
+        for number, stage in enumerate(stages):
+            if 0 <= tick - number < CHUNKS:
+                stage(tick - number)
+    sends += list(flying.values()) + wg_copies
+
+    @pl.loop(0, DEVICES)
+    def _(i):
+        rows = pl.ds(pl.multiple_of(i * rows8, rows8), rows8)
+        ids8 = ids_ref[rows, :] - first
+        lane = lax.broadcasted_iota(jnp.int32, (rows8, lanes), 1)
+        row = row_of(i)
+        value = jnp.zeros((rows8, lanes), jnp.float32)
+        for f in range(plane_feat // lanes):
+            at = ids8 - f * lanes
+            inside = (at >= 0) & (at < lanes)
+            at = jnp.clip(at, 0, lanes - 1)
+            taken = []
+            for batch in range(2):
+                block = back[
+                    pl.ds(pl.multiple_of(row + batch * rows8, rows8), rows8),
+                    f * lanes : (f + 1) * lanes,
+                ]
+                taken.append(
+                    jnp.take_along_axis(block, at, axis=1, mode="promise_in_bounds")
+                )
+            found = jnp.where(lane < top_k, taken[0], taken[1])
+            value = jnp.where(inside, found, value)
+        pick[rows, :] = value
+
+    to_owner = []
+    for r in range(1, DEVICES):
+        owner = lax.rem(me + r, DEVICES)
+        to_owner.append(
+            remote(
+                pick.at[span(owner * rows8, rows8), :],
+                cg_got.at[r],
+                cg_send.at[0, r],
+                cg_recv.at[0, r],
+                owner,
+            )
+        )
+    for copy in to_owner:
+        copy.wait_recv()
+    my_rows = span(me * rows8, rows8)
+    total = pick[my_rows, :]
+    for r in range(1, DEVICES):
+        total = total + cg_got[r]
+    cg_out[my_rows, :] = total
+    to_all = []
+    for r in range(1, DEVICES):
+        to_all.append(
+            remote(
+                cg_out.at[my_rows, :],
+                cg_out.at[my_rows, :],
+                cg_send.at[1, r],
+                cg_recv.at[1, r],
+                lax.rem(me + r, DEVICES),
+            )
+        )
+    for copy in to_all + wg_copies:
+        copy.wait_recv()
+    for copy in wg_local:
+        copy.wait()
+    for copy in sends + to_owner + to_all:
+        copy.wait_send()
+
+
+def fused(residual, feature_ids, activations, decoder, bias):
+    feat, model_width = decoder.shape
+    batches, share_rows = residual.shape[0], residual.shape[1]
+    tokens = feature_ids.shape[1]
+    width = model_width // QUARTERS
+    rows = batches * tokens
+    ids = jnp.concatenate([feature_ids[0], feature_ids[1]], axis=1)
+    acts = jnp.concatenate([activations[0], activations[1]], axis=1).astype(jnp.float32)
+    lanes = ids.shape[1]
+    vmem = pl.BlockSpec(memory_space=pltpu.VMEM)
+    hbm = pl.BlockSpec(memory_space=pl.ANY)
+    weight_grad, grads = pl.pallas_call(
+        fused_kernel,
+        out_shape=(
+            jax.ShapeDtypeStruct((feat, model_width), jnp.bfloat16),
+            jax.ShapeDtypeStruct((tokens, lanes), jnp.float32),
+        ),
+        in_specs=[vmem, vmem, vmem, hbm, vmem],
+        out_specs=(hbm, vmem),
+        scratch_shapes=[
+            pltpu.VMEM((QUARTERS * feat, width), jnp.bfloat16),
+            pltpu.VMEM((rows, width), SUM_TYPE),
+            pltpu.VMEM((rows // 2, width), SUM_TYPE),
+            pltpu.VMEM((rows // 4, width), SUM_TYPE),
+            pltpu.VMEM((rows, width), jnp.bfloat16),
+            pltpu.VMEM((QUARTERS * feat, width), jnp.bfloat16),
+            pltpu.VMEM((rows // 4, width), jnp.bfloat16),
+            pltpu.VMEM((rows, QUARTERS * feat), jnp.bfloat16),
+            pltpu.VMEM((QUARTERS * feat, rows), jnp.bfloat16),
+            pltpu.VMEM((rows, QUARTERS * feat), jnp.float32),
+            pltpu.VMEM((tokens, lanes), jnp.float32),
+            pltpu.VMEM((DEVICES, share_rows, lanes), jnp.float32),
+            pltpu.SemaphoreType.DMA((2,)),
+            pltpu.SemaphoreType.DMA((CHUNKS, QUARTERS)),
+            pltpu.SemaphoreType.DMA((CHUNKS, QUARTERS)),
+            pltpu.SemaphoreType.DMA((QUARTERS,)),
+            pltpu.SemaphoreType.DMA((QUARTERS,)),
+            pltpu.SemaphoreType.DMA((4, CHUNKS)),
+            pltpu.SemaphoreType.DMA((4, CHUNKS)),
+            pltpu.SemaphoreType.DMA((CHUNKS, QUARTERS)),
+            pltpu.SemaphoreType.DMA((CHUNKS, QUARTERS)),
+            pltpu.SemaphoreType.DMA((CHUNKS,)),
+            pltpu.SemaphoreType.DMA((2, DEVICES)),
+            pltpu.SemaphoreType.DMA((2, DEVICES)),
+        ],
+        compiler_params=pltpu.CompilerParams(
+            collective_id=0, has_side_effects=True, vmem_limit_bytes=40 * 2**20
+        ),
+        name="fused_backward",
+    )(
+        ids,
+        acts,
+        residual.reshape(batches * share_rows, model_width),
+        decoder,
+        bias.astype(jnp.float32).reshape(1, model_width),
+    )
+    code_grad = grads.reshape(tokens, batches, lanes // batches).transpose(1, 0, 2)
+    return weight_grad, code_grad
 
 
 def local_codes(ids_block, acts_block, first_feature, feat_count):
@@ -68,7 +426,7 @@
         P("groups"),
     )
     return jax.shard_map(
-        local,
+        fused if mesh.shape["feat"] == DEVICES else local,
         mesh=mesh,
         in_specs=placed,
         out_specs=(P(("groups", "feat"), None), P(None, "groups", None)),

time: 410 us -> 96.1 us (0.23)
  waiting for transfers between devices: 268 us -> 0 us
  local copies, waits for them, and re-layouts: 105 us -> 6.52 us
  Pallas kernels: 0 us -> 87.6 us
  matrix products: 18.1 us -> 0 us
  between operations: 13.9 us -> 0.68 us
    reduce_scatter x2 -> x0, waiting for transfers between devices: 146 us -> none  [local(): lax.psum_scatter(project(jnp.int32(0), share_rows * lax.axis_size('feat')...]
    gather x6 -> x0, local copies, waits for them, and re-layouts: 102 us -> none  [pick_owned(): jnp.take_along_axis(backward, jnp.clip(local_ids, 0, feat_count - 1), axi...]
    pallas_call x0 -> x1, Pallas kernels: none -> 87.6 us  [fused(): pl.pallas_call(fused_kernel, out_shape=(jax.ShapeDtypeStruct((feat, model...]
    psum x1 -> x0, waiting for transfers between devices: 81.3 us -> none  [local(): code_grad = lax.psum(jnp.stack(picks), 'feat')]
    all_gather x2 -> x0, waiting for transfers between devices: 40.1 us -> none  [local(): errors_all = lax.all_gather(error_share, 'feat', axis=0, tiled=True)]
    dot_general x8 -> x0, matrix products: 18.1 us -> none  [the longest x2 5.34 us: project(): return jnp.dot(codes, decoder, preferred_element_type=jnp.float32)]
  transfers between devices with their start and end apart: 5 -> 0, of which waited for: 4 -> 0; matrix products, arithmetic and copies ran while one was open for 15% -> 0% of each run, Pallas kernels for 0% -> 0%
where the time goes in v1:
time: 96.1 us; the launch traced here: 95.7 us
  Pallas kernels  87.6 us (91%)
  local copies, waits for them, and re-layouts  6.52 us (7%)
    pallas_call x1, Pallas kernels, fused(): pl.pallas_call(fused_kernel, out_shape=(jax.ShapeDtypeStruct((feat, model...  87.6 us
    unnamed x9, local copies, waits for them, and re-layouts  4.27 us

profile of v1, /device:TPU:0, one launch (start us, length us, event | category | flops | bytes accessed | tf_op | source)
XLA Modules:
  0.0 95.7 jit_solution(5439367267133493860)
XLA Ops:
  0.6 0.7 reshape.19
  1.4 0.7 fusion.1
  2.1 0.1 copy.19
  2.2 0.1 copy.20
  2.3 0.1 maximum_convert_fusion.acts_ref
  2.4 0.8 fusion
  3.2 0.1 copy.17
  3.3 0.1 copy.18
  3.4 0.1 pad_add_fusion.ids_ref
  3.5 0.0 copy-start
  3.5 1.6 %copy-done = bf16[128,8192]{1,0:T(8,128)(2,1)S(1)} copy-done((bf16[128,8192]{1,0:T(8,128)(2,1)S(1)}, bf16[128,8192]{1,0:T(8,128)(2,1)}, u32[]{:S(2)}) %copy-start) | copy-done | bytes 2097176
  5.1 0.0 copy-start.1
  5.1 0.9 copy-done.1
  6.0 87.6 %fused_backward.1 = (bf16[128,8192]{1,0:T(8,128)(2,1)S(1)}, f32[128,128]{1,0:T(8,128)S(1)}) custom-call(s32[128,128]{1,0:T(8,128)S(1)} %pad_add_fusion.ids_ref, f32[128,128]{1,0:T(8,128)S(1)} %maximum_convert_fusion.acts_ref, bf16[16,8192]{1,0:T(8,128)(2,1)S(1)} %bitcast.9, bf16[128,8192]{1,0:T(8,128)(2,1)S(1)} %copy-done, f32[1,8192]{1,0:T(1,128)S(1)} %bitcast.10), custom_call_target="tpu_custom_call" | custom-call | tf_op jit(solution)/shard_map/fused_backward/pallas_call | solution.py:316
  93.6 0.7 copy.16
  94.4 1.3 %copy.22 = bf16[128,8192]{1,0:T(8,128)(2,1)} copy(bf16[128,8192]{1,0:T(8,128)(2,1)S(1)} %get-tuple-element.12) | data formatting | bytes 4194304
Async XLA Ops:
  3.5 1.6 %copy-start = (bf16[128,8192]{1,0:T(8,128)(2,1)S(1)}, bf16[128,8192]{1,0:T(8,128)(2,1)}, u32[]{:S(2)}) copy-start(bf16[128,8192]{1,0:T(8,128)(2,1)} %dec_in.1) | copy-start | bytes 6291460
  5.1 0.9 copy-start.1

commit v2 on v1

--- a/solution.py
+++ b/solution.py
@@ -9,7 +9,8 @@
 PLANES = 4
 QUARTERS = 4
 DEVICES = PLANES * QUARTERS
-CHUNKS = 4
+CHUNKS = 8
+LAGS = (0, 1, 2, 3, 4)
 SUM_TYPE = jnp.float32
 
 
@@ -140,11 +141,6 @@
         both = jnp.concatenate(blocks, axis=0)
         codes[pl.ds(row_of(i), share), :] = both.astype(jnp.bfloat16)
 
-    for f in range(QUARTERS):
-        codes_t[f * feat : (f + 1) * feat, :] = (
-            codes[:, f * feat : (f + 1) * feat].astype(jnp.float32).T.astype(jnp.bfloat16)
-        )
-
     own_dec.wait()
     own_res.wait()
 
@@ -233,11 +229,19 @@
         )
         back[...] = term if c == 0 else back[...] + term
 
+    def transpose_codes():
+        for f in range(QUARTERS):
+            codes_t[f * feat : (f + 1) * feat, :] = (
+                codes[:, f * feat : (f + 1) * feat].astype(jnp.float32).T.astype(jnp.bfloat16)
+            )
+
     stages = (project, halve, make_error, spread, gradients)
-    for tick in range(CHUNKS + len(stages) - 1):
-        for number, stage in enumerate(stages):
-            if 0 <= tick - number < CHUNKS:
-                stage(tick - number)
+    for tick in range(CHUNKS + LAGS[-1]):
+        if tick == 1:
+            transpose_codes()
+        for lag, stage in zip(LAGS, stages):
+            if 0 <= tick - lag < CHUNKS:
+                stage(tick - lag)
     sends += list(flying.values()) + wg_copies
 
     @pl.loop(0, DEVICES)
@@ -319,7 +323,7 @@
             jax.ShapeDtypeStruct((feat, model_width), jnp.bfloat16),
             jax.ShapeDtypeStruct((tokens, lanes), jnp.float32),
         ),
-        in_specs=[vmem, vmem, vmem, hbm, vmem],
+        in_specs=[vmem, vmem, hbm, hbm, vmem],
         out_specs=(hbm, vmem),
         scratch_shapes=[
             pltpu.VMEM((QUARTERS * feat, width), jnp.bfloat16),

time: 96.1 us -> 92.6 us (0.964)
  Pallas kernels: 87.6 us -> 84.1 us
    pallas_call x1, Pallas kernels: 87.6 us -> 84.1 us  [fused(): pl.pallas_call(fused_kernel, out_shape=(jax.ShapeDtypeStruct((feat, model...]
where the time goes in v2:
time: 92.6 us; the launch traced here: 92.2 us
  Pallas kernels  84.1 us (91%)
  local copies, waits for them, and re-layouts  6.52 us (7%)
    pallas_call x1, Pallas kernels, fused(): pl.pallas_call(fused_kernel, out_shape=(jax.ShapeDtypeStruct((feat, model...  84.1 us
    unnamed x9, local copies, waits for them, and re-layouts  4.27 us

profile of v2, /device:TPU:0, one launch (start us, length us, event | category | flops | bytes accessed | tf_op | source)
XLA Modules:
  0.0 92.2 jit_solution(13535023556014388405)
XLA Ops:
  0.6 0.7 reshape.19
  1.4 0.7 fusion.1
  2.1 0.1 copy.19
  2.2 0.1 copy.20
  2.3 0.1 maximum_convert_fusion.acts_ref
  2.4 0.8 fusion
  3.2 0.1 copy.17
  3.3 0.1 copy.18
  3.4 0.1 pad_add_fusion.ids_ref
  3.5 0.0 copy-start
  3.5 1.6 %copy-done = bf16[128,8192]{1,0:T(8,128)(2,1)S(1)} copy-done((bf16[128,8192]{1,0:T(8,128)(2,1)S(1)}, bf16[128,8192]{1,0:T(8,128)(2,1)}, u32[]{:S(2)}) %copy-start) | copy-done | bytes 2097176
  5.1 0.0 copy-start.1
  5.1 0.9 %copy-done.1 = bf16[2,8,8192]{2,1,0:T(8,128)(2,1)S(1)} copy-done((bf16[2,8,8192]{2,1,0:T(8,128)(2,1)S(1)}, bf16[2,8,8192]{2,1,0:T(8,128)(2,1)}, u32[]{:S(2)}) %copy-start.1) | copy-done | bytes 262168
  6.0 84.1 %fused_backward.1 = (bf16[128,8192]{1,0:T(8,128)(2,1)S(1)}, f32[128,128]{1,0:T(8,128)S(1)}) custom-call(s32[128,128]{1,0:T(8,128)S(1)} %pad_add_fusion.ids_ref, f32[128,128]{1,0:T(8,128)S(1)} %maximum_convert_fusion.acts_ref, bf16[16,8192]{1,0:T(8,128)(2,1)S(1)} %bitcast.9, bf16[128,8192]{1,0:T(8,128)(2,1)S(1)} %copy-done, f32[1,8192]{1,0:T(1,128)S(1)} %bitcast.10), custom_call_target="tpu_custom_call" | custom-call | tf_op jit(solution)/shard_map/fused_backward/pallas_call | solution.py:320
  90.1 0.7 copy.16
  90.9 1.3 %copy.22 = bf16[128,8192]{1,0:T(8,128)(2,1)} copy(bf16[128,8192]{1,0:T(8,128)(2,1)S(1)} %get-tuple-element.12) | data formatting | bytes 4194304
Async XLA Ops:
  3.5 1.6 %copy-start = (bf16[128,8192]{1,0:T(8,128)(2,1)S(1)}, bf16[128,8192]{1,0:T(8,128)(2,1)}, u32[]{:S(2)}) copy-start(bf16[128,8192]{1,0:T(8,128)(2,1)} %dec_in.1) | copy-start | bytes 6291460
  5.1 0.9 %copy-start.1 = (bf16[2,8,8192]{2,1,0:T(8,128)(2,1)S(1)}, bf16[2,8,8192]{2,1,0:T(8,128)(2,1)}, u32[]{:S(2)}) copy-start(bf16[2,8,8192]{2,1,0:T(8,128)(2,1)} %param.5) | copy-start | bytes 786436

commit v3 on v2

--- a/solution.py
+++ b/solution.py
@@ -10,7 +10,7 @@
 QUARTERS = 4
 DEVICES = PLANES * QUARTERS
 CHUNKS = 8
-LAGS = (0, 1, 2, 3, 4)
+LAGS = (0, 1, 2, 3, 4, 5, 6)
 SUM_TYPE = jnp.float32
 
 
@@ -26,6 +26,7 @@
     part,
     got1,
     got2,
+    got3,
     err,
     wg,
     res,
@@ -59,9 +60,10 @@
 
     me = lax.axis_index("feat")
     z, q = lax.div(me, QUARTERS), lax.rem(me, QUARTERS)
-    z_hi, z_lo = lax.div(z, 2), lax.rem(z, 2)
+    side, z_lo = lax.div(z, 2), lax.rem(z, 2)
+    inner = lax.rem(z_lo + side, 2)
     near = (z + 1 - 2 * z_lo) * QUARTERS + q
-    far = lax.rem(z + 2, PLANES) * QUARTERS + q
+    across = (PLANES - 1 - z) * QUARTERS + q
     mates = [lax.rem(q + r, QUARTERS) for r in range(QUARTERS)]
 
     def span(start, size):
@@ -124,7 +126,9 @@
 
     def row_of(i):
         zi, qi = lax.div(i, QUARTERS), lax.rem(i, QUARTERS)
-        return pl.multiple_of((lax.rem(zi, 2) * 2 + lax.div(zi, 2)) * quarter + qi * share, share)
+        side_i = lax.div(zi, 2)
+        block = side_i * 2 + lax.rem(lax.rem(zi, 2) + side_i, 2)
+        return pl.multiple_of(block * quarter + qi * share, share)
 
     @pl.loop(0, DEVICES)
     def _(i):
@@ -144,64 +148,116 @@
     own_dec.wait()
     own_res.wait()
 
-    mine_half = span(z_lo * half, half)
-    other_half = span((1 - z_lo) * half, half)
-    mine = span(z_lo * half + z_hi * quarter, quarter)
-    other = span(z_lo * half + (1 - z_hi) * quarter, quarter)
-    flying = {}
+    mine_half = span(side * half, half)
+    other_half = span((1 - side) * half, half)
+    end_rows = span(side * half, quarter)
+    inner_rows = span(side * half + quarter, quarter)
+    mine = span(side * half + inner * quarter, quarter)
 
     def cols_of(c):
         return pl.ds(c * step, step)
 
+    def along(kind, c):
+        cols = cols_of(c)
+        src, dst, device = (
+            (part.at[other_half, cols], got1.at[pl.ds(0, half), cols], near),
+            (part.at[inner_rows, cols], got1.at[pl.ds(half, quarter), cols], near),
+            (part.at[other_half, cols], got2.at[:, cols], across),
+            (part.at[end_rows, cols], got3.at[:, cols], near),
+            (err.at[inner_rows, cols], err.at[inner_rows, cols], across),
+            (err.at[inner_rows, cols], err.at[inner_rows, cols], near),
+            (err.at[end_rows, cols], err.at[end_rows, cols], near),
+            (err.at[end_rows, cols], err.at[end_rows, cols], across),
+            (err.at[other_half, cols], err.at[other_half, cols], near),
+        )[kind]
+        return pltpu.make_async_remote_copy(
+            src_ref=src,
+            dst_ref=dst,
+            send_sem=sum_send.at[kind, c],
+            recv_sem=sum_recv.at[kind, c],
+            device_id={"feat": device},
+            device_id_type=MESH,
+        )
+
+    SUM_HALF, SUM_INNER, SUM_ACROSS, SUM_BACK = 0, 1, 2, 3
+    ERR_ACROSS, ERR_NEAR, ERR_END, ERR_END_ACROSS, ERR_REST = 4, 5, 6, 7, 8
+    FROM_END = (SUM_HALF, SUM_INNER, ERR_END)
+    FROM_INNER = (SUM_ACROSS, SUM_BACK, ERR_ACROSS, ERR_NEAR, ERR_END_ACROSS, ERR_REST)
+
     def project(c):
         cols = cols_of(c)
         for r in range(1, QUARTERS):
             dec_copies[c, r].wait_recv()
-        part[:, cols] = jnp.dot(
-            codes[...], dec[:, cols], preferred_element_type=jnp.float32
-        ).astype(part.dtype)
-        flying[0, c] = remote(
-            part.at[other_half, cols], got1.at[:, cols], sum_send.at[0, c], sum_recv.at[0, c], near
-        )
-
-    def halve(c):
-        cols = cols_of(c)
-        flying[0, c].wait_recv()
-        part[mine_half, cols] = part[mine_half, cols] + got1[:, cols]
-        flying[1, c] = remote(
-            part.at[other, cols], got2.at[:, cols], sum_send.at[1, c], sum_recv.at[1, c], far
-        )
-
-    def make_error(c):
+        part[:, cols] = jnp.dot(codes[...], dec[:, cols], preferred_element_type=jnp.float32)
+
+        @pl.when(inner == 0)
+        def _():
+            along(SUM_HALF, c).start()
+            along(SUM_INNER, c).start()
+
+    def pass_on(c):
+        cols = cols_of(c)
+
+        @pl.when(inner == 1)
+        def _():
+            along(SUM_HALF, c).wait_recv()
+            part[other_half, cols] = part[other_half, cols] + got1[:half, cols]
+            along(SUM_ACROSS, c).start()
+
+    def round_error(recon, c):
+        cols = cols_of(c)
+        shift = bias_ref[:, span(q * width + c * step, step)]
+        err[mine, cols] = (recon + shift - res[:, cols].astype(jnp.float32)).astype(jnp.bfloat16)
+
+    def finish_inner(c):
         cols = cols_of(c)
         if c == 0:
             for copy in res_copies:
                 copy.wait_recv()
-        flying[1, c].wait_recv()
-        recon = part[mine, cols] + got2[:, cols]
-        shift = bias_ref[:, span(q * width + c * step, step)]
-        err[mine, cols] = (recon + shift - res[:, cols].astype(jnp.float32)).astype(jnp.bfloat16)
-        flying[2, c] = remote(
-            err.at[mine, cols], err.at[mine, cols], sum_send.at[2, c], sum_recv.at[2, c], far
-        )
-
-    def spread(c):
-        cols = cols_of(c)
-        flying[2, c].wait_recv()
-        flying[3, c] = remote(
-            err.at[mine_half, cols],
-            err.at[mine_half, cols],
-            sum_send.at[3, c],
-            sum_recv.at[3, c],
-            near,
-        )
+
+        @pl.when(inner == 1)
+        def _():
+            along(SUM_ACROSS, c).wait_recv()
+            part[end_rows, cols] = part[end_rows, cols] + got2[:quarter, cols]
+            along(SUM_BACK, c).start()
+            along(SUM_INNER, c).wait_recv()
+            round_error(part[inner_rows, cols] + got1[half:, cols] + got2[quarter:, cols], c)
+            along(ERR_ACROSS, c).start()
+            along(ERR_NEAR, c).start()
+
+    def finish_end(c):
+        cols = cols_of(c)
+
+        @pl.when(inner == 0)
+        def _():
+            along(SUM_BACK, c).wait_recv()
+            round_error(part[end_rows, cols] + got3[:, cols], c)
+            along(ERR_END, c).start()
+
+    def send_across(c):
+        @pl.when(inner == 1)
+        def _():
+            along(ERR_END, c).wait_recv()
+            along(ERR_END_ACROSS, c).start()
+
+    def send_back(c):
+        @pl.when(inner == 1)
+        def _():
+            along(ERR_ACROSS, c).wait_recv()
+            along(ERR_END_ACROSS, c).wait_recv()
+            along(ERR_REST, c).start()
 
     wg_copies = []
     wg_local = []
 
     def gradients(c):
         cols = cols_of(c)
-        flying[3, c].wait_recv()
+
+        @pl.when(inner == 0)
+        def _():
+            along(ERR_NEAR, c).wait_recv()
+            along(ERR_REST, c).wait_recv()
+
         wg[:, cols] = jnp.dot(
             codes_t[...], err[:, cols], preferred_element_type=jnp.float32
         ).astype(jnp.bfloat16)
@@ -235,14 +291,14 @@
                 codes[:, f * feat : (f + 1) * feat].astype(jnp.float32).T.astype(jnp.bfloat16)
             )
 
-    stages = (project, halve, make_error, spread, gradients)
+    stages = (project, pass_on, finish_inner, finish_end, send_across, send_back, gradients)
     for tick in range(CHUNKS + LAGS[-1]):
         if tick == 1:
             transpose_codes()
         for lag, stage in zip(LAGS, stages):
             if 0 <= tick - lag < CHUNKS:
                 stage(tick - lag)
-    sends += list(flying.values()) + wg_copies
+    sends += wg_copies
 
     @pl.loop(0, DEVICES)
     def _(i):
@@ -305,6 +361,18 @@
     for copy in sends + to_owner + to_all:
         copy.wait_send()
 
+    @pl.when(inner == 0)
+    def _():
+        for kind in FROM_END:
+            for c in range(CHUNKS):
+                along(kind, c).wait_send()
+
+    @pl.when(inner == 1)
+    def _():
+        for kind in FROM_INNER:
+            for c in range(CHUNKS):
+                along(kind, c).wait_send()
+
 
 def fused(residual, feature_ids, activations, decoder, bias):
     feat, model_width = decoder.shape
@@ -328,6 +396,7 @@
         scratch_shapes=[
             pltpu.VMEM((QUARTERS * feat, width), jnp.bfloat16),
             pltpu.VMEM((rows, width), SUM_TYPE),
+            pltpu.VMEM((3 * rows // 4, width), SUM_TYPE),
             pltpu.VMEM((rows // 2, width), SUM_TYPE),
             pltpu.VMEM((rows // 4, width), SUM_TYPE),
             pltpu.VMEM((rows, width), jnp.bfloat16),
@@ -343,8 +412,8 @@
             pltpu.SemaphoreType.DMA((CHUNKS, QUARTERS)),
             pltpu.SemaphoreType.DMA((QUARTERS,)),
             pltpu.SemaphoreType.DMA((QUARTERS,)),
-            pltpu.SemaphoreType.DMA((4, CHUNKS)),
-            pltpu.SemaphoreType.DMA((4, CHUNKS)),
+            pltpu.SemaphoreType.DMA((9, CHUNKS)),
+            pltpu.SemaphoreType.DMA((9, CHUNKS)),
             pltpu.SemaphoreType.DMA((CHUNKS, QUARTERS)),
             pltpu.SemaphoreType.DMA((CHUNKS, QUARTERS)),
             pltpu.SemaphoreType.DMA((CHUNKS,)),

time: 92.6 us -> 92.6 us (level)
  no operation moved by 1% of the time
where the time goes in v3:
time: 92.6 us; the launch traced here: 92.2 us
  Pallas kernels  84.1 us (91%)
  local copies, waits for them, and re-layouts  6.52 us (7%)
    pallas_call x1, Pallas kernels, fused(): pl.pallas_call(fused_kernel, out_shape=(jax.ShapeDtypeStruct((feat, model...  84.1 us
    unnamed x9, local copies, waits for them, and re-layouts  4.27 us

profile of v3, /device:TPU:0, one launch (start us, length us, event | category | flops | bytes accessed | tf_op | source)
XLA Modules:
  0.0 92.2 jit_solution(11068976967636546509)
XLA Ops:
  0.6 0.7 reshape.19
  1.4 0.7 fusion.1
  2.1 0.1 copy.19
  2.2 0.1 copy.20
  2.3 0.1 maximum_convert_fusion.acts_ref
  2.4 0.8 fusion
  3.2 0.1 copy.17
  3.3 0.1 copy.18
  3.4 0.1 pad_add_fusion.ids_ref
  3.5 0.0 copy-start
  3.5 1.6 %copy-done = bf16[128,8192]{1,0:T(8,128)(2,1)S(1)} copy-done((bf16[128,8192]{1,0:T(8,128)(2,1)S(1)}, bf16[128,8192]{1,0:T(8,128)(2,1)}, u32[]{:S(2)}) %copy-start) | copy-done | bytes 2097176
  5.1 0.0 copy-start.1
  5.1 0.9 %copy-done.1 = bf16[2,8,8192]{2,1,0:T(8,128)(2,1)S(1)} copy-done((bf16[2,8,8192]{2,1,0:T(8,128)(2,1)S(1)}, bf16[2,8,8192]{2,1,0:T(8,128)(2,1)}, u32[]{:S(2)}) %copy-start.1) | copy-done | bytes 262168
  6.0 84.1 %fused_backward.1 = (bf16[128,8192]{1,0:T(8,128)(2,1)S(1)}, f32[128,128]{1,0:T(8,128)S(1)}) custom-call(s32[128,128]{1,0:T(8,128)S(1)} %pad_add_fusion.ids_ref, f32[128,128]{1,0:T(8,128)S(1)} %maximum_convert_fusion.acts_ref, bf16[16,8192]{1,0:T(8,128)(2,1)S(1)} %bitcast.9, bf16[128,8192]{1,0:T(8,128)(2,1)S(1)} %copy-done, f32[1,8192]{1,0:T(1,128)S(1)} %bitcast.10), custom_call_target="tpu_custom_call" | custom-call | tf_op jit(solution)/shard_map/fused_backward/pallas_call | solution.py:388
  90.1 0.7 copy.16
  90.9 1.3 %copy.22 = bf16[128,8192]{1,0:T(8,128)(2,1)} copy(bf16[128,8192]{1,0:T(8,128)(2,1)S(1)} %get-tuple-element.12) | data formatting | bytes 4194304
Async XLA Ops:
  3.5 1.6 %copy-start = (bf16[128,8192]{1,0:T(8,128)(2,1)S(1)}, bf16[128,8192]{1,0:T(8,128)(2,1)}, u32[]{:S(2)}) copy-start(bf16[128,8192]{1,0:T(8,128)(2,1)} %dec_in.1) | copy-start | bytes 6291460
  5.1 0.9 %copy-start.1 = (bf16[2,8,8192]{2,1,0:T(8,128)(2,1)S(1)}, bf16[2,8,8192]{2,1,0:T(8,128)(2,1)}, u32[]{:S(2)}) copy-start(bf16[2,8,8192]{2,1,0:T(8,128)(2,1)} %param.5) | copy-start | bytes 786436
